TPU v7x, 128 devices: a whole 4x4x4 slice. The times are simulated.
128 devices in a mesh: peer: 32 (over x, y_hi, z), chan: 4 (over y_lo, core).
Axes of the slice: x: 4, y: 4 (y_hi: 2, y_lo: 2; y = y_hi * 2 + y_lo), z: 4, core: 2. Of those that a mesh axis runs over, the one named last changes fastest.
Arguments:
- images: bfloat16 [2, 64, 14, 14, 512], P(None, 'peer', None, None, 'chan'), may hold values from -12 to 12
- cotangent: bfloat16 [2, 32, 4, 14, 14, 512], P(None, 'peer', None, None, None, 'chan'), may hold values from -6 to 6
- image_ids: int32 [2, 32, 4], P(None, 'peer'), may hold values from 0 to 63, as said below
- counts: int32 [2, 32], P(None, 'peer'), may hold values from 1 to 4, 64 in all within a row
- hop_exponents: int32 [2], replicated, may hold values from 0 to 2
- param_mats: float32 [32, 2, 512, 2048], P('peer', None, None, 'chan'), may hold values from -0.25 to 0.25
- param_chans: float32 [32, 54, 512], P('peer', None, 'chan'), may hold values from -3 to 3
- param_bias: float32 [32, 2048], P('peer', 'chan'), may hold values from -3 to 3
- track_mats: float32 [32, 2, 512, 2048], P('peer', None, None, 'chan'), may hold values from -6 to 6
- track_chans: float32 [32, 54, 512], P('peer', None, 'chan'), may hold values from -6 to 6
- track_bias: float32 [32, 2048], P('peer', 'chan'), may hold values from -6 to 6
- grad_mats: float32 [32, 2, 512, 2048], P('peer', None, None, 'chan'), may hold values from -6 to 6
- grad_chans: float32 [32, 54, 512], P('peer', None, 'chan'), may hold values from -6 to 6
- grad_bias: float32 [32, 2048], P('peer', 'chan'), may hold values from -6 to 6
Outputs:
- new_param_mats: float32 [32, 2, 512, 2048], P('peer', None, None, 'chan')
- new_param_chans: float32 [32, 54, 512], P('peer', None, 'chan')
- new_param_bias: float32 [32, 2048], P('peer', 'chan')
- new_track_mats: float32 [32, 2, 512, 2048], P('peer', None, None, 'chan')
- new_track_chans: float32 [32, 54, 512], P('peer', None, 'chan')
- new_track_bias: float32 [32, 2048], P('peer', 'chan')
Inputs may be any that keep to these rules, and one draw needn't show every extreme that they name: `image_ids`: entry s of a worker's list is read only where s is below its count; in each worker's list at most 2 entries name rows of one loader shard (rows b * 2 to (b + 1) * 2 - 1), and in every iteration some list has exactly 2 such entries. `counts`: in every iteration some worker has all 4 entries live.
All inputs are finite; a program needn't handle non-finite values. No bound on the sum of `counts` on one device may be relied on, other than what follows from the above.
Results may differ from a plain program's by a relative error of at most 0.006.
Values may be sent and summed in bfloat16 or wider, within the bound.
A program may use at most 128 MiB of HBM per device.

v0:
```python
import jax
import jax.numpy as jnp
from jax import lax
from jax.sharding import PartitionSpec as P

KS = 7
ITERS = 2


EPS = 1e-06
LEARNING_RATE = 0.01


def partner(value, axis, stride):
    return lax.ppermute(value, axis, [(i, i ^ 1 << stride) for i in range(lax.axis_size(axis))])


def gelu_parts(hidden):
    normal_cdf = 0.5 * (1.0 + jax.scipy.special.erf(hidden * 0.7071067811865476))
    density = jnp.exp(-0.5 * hidden * hidden) * 0.3989422804014327
    return (hidden * normal_cdf, normal_cdf + hidden * density)


def pad_maps(source):
    half = KS // 2
    return jnp.pad(source, ((0, 0), (half, half), (half, half), (0, 0)))


def depthwise(source, kernel):
    padded = pad_maps(source)
    height, feature_width = (source.shape[1], source.shape[2])
    total = jnp.zeros(source.shape, jnp.float32)
    for row_off in range(KS):
        for col_off in range(KS):
            window = padded[
                :, row_off : row_off + height, col_off : col_off + feature_width, :
            ].astype(jnp.float32)
            total = total + window * kernel[row_off * KS + col_off]
    return total


def kernel_grad(source, grad_conv):
    padded = pad_maps(source)
    height, feature_width = (source.shape[1], source.shape[2])
    pieces = []
    for row_off in range(KS):
        for col_off in range(KS):
            window = padded[
                :, row_off : row_off + height, col_off : col_off + feature_width, :
            ].astype(jnp.float32)
            pieces.append(jnp.sum(window * grad_conv, (0, 1, 2)))
    return jnp.stack(pieces, 0)


def hop_switch(hop, branches, operand):
    return lax.switch(jnp.clip(hop, 0, len(branches) - 1), branches, operand)


def swap_joint(values, hop):
    levels = lax.axis_size("peer").bit_length() - 1

    def make_branch(bit_index):
        return lambda current: partner(current, "peer", bit_index)

    return hop_switch(hop, [make_branch(bit_index) for bit_index in range(levels)], values)


def fetch_images(images_now, slot_ids, valid):
    blocks = images_now.shape[0]
    row_size = images_now.shape[1] * images_now.shape[2] * images_now.shape[3]
    flat_images = images_now.reshape(blocks, row_size)
    piece = lax.all_gather(flat_images, "peer", axis=0, tiled=True)
    piece_rows = piece.shape[0]
    selected = (slot_ids[:, None] == jnp.arange(piece_rows, dtype=jnp.int32)[None, :]) & valid[
        :, None
    ]
    gathered = jnp.dot(selected.astype(jnp.bfloat16), piece, preferred_element_type=jnp.float32)
    return gathered.astype(jnp.bfloat16)


def local_grad(flattened, layout, images_now, cot_slots, slot_ids, slot_count):
    mats_shape, rows_shape, hid_width = layout
    mats_size = mats_shape[0] * mats_shape[1] * mats_shape[2]
    rows_size = rows_shape[0] * rows_shape[1]
    matrices = flattened[:mats_size].reshape(mats_shape)
    channel_row_block = flattened[mats_size : mats_size + rows_size].reshape(rows_shape)
    hidden_bias = flattened[mats_size + rows_size :]
    filter_weight = KS * KS
    slots = slot_ids.shape[0]
    height, feature_width = (images_now.shape[1], images_now.shape[2])
    chan_width = images_now.shape[3]
    full_width = matrices.shape[1]
    valid = jnp.arange(slots, dtype=jnp.int32) < slot_count
    picked = fetch_images(images_now, slot_ids, valid).reshape(
        slots, height, feature_width, chan_width
    )
    conv_out = (
        depthwise(picked, channel_row_block[:filter_weight]) + channel_row_block[filter_weight]
    ).reshape(-1, chan_width)
    average = lax.psum(jnp.sum(conv_out, 1), "chan") / full_width
    mean_removed = conv_out - average[:, None]
    variance = lax.psum(jnp.sum(mean_removed * mean_removed, 1), "chan") / full_width
    inverse_deviation = lax.rsqrt(variance + EPS)
    standardized_input = mean_removed * inverse_deviation[:, None]
    norm_scale = channel_row_block[filter_weight + 1]
    normalized_rows = (
        standardized_input * norm_scale + channel_row_block[filter_weight + 2]
    ).astype(jnp.bfloat16)
    normed_full = lax.all_gather(normalized_rows, "chan", axis=1, tiled=True)
    w_first = matrices[0].astype(jnp.bfloat16)
    w_second = matrices[1].astype(jnp.bfloat16)
    hidden = jnp.dot(normed_full, w_first, preferred_element_type=jnp.float32) + hidden_bias
    act_full, slope = gelu_parts(hidden)
    activated = act_full.astype(jnp.bfloat16)
    partial_out = lax.dot_general(
        activated, w_second, (((1,), (1,)), ((), ())), preferred_element_type=jnp.float32
    )
    branch = (
        lax.psum_scatter(partial_out, "chan", scatter_dimension=1, tiled=True)
        + channel_row_block[filter_weight + 3]
    )
    slot_weight = valid.astype(jnp.float32) / slot_count.astype(jnp.float32)
    weighted = (cot_slots.astype(jnp.float32) * slot_weight[:, None, None, None]).reshape(
        -1, chan_width
    )
    layer_scale = channel_row_block[filter_weight + 4]
    grad_scale = jnp.sum(weighted * branch, 0)
    dbranch = layer_scale * weighted
    grad_bout = jnp.sum(dbranch, 0)
    dbranch_full = lax.all_gather(dbranch.astype(jnp.bfloat16), "chan", axis=1, tiled=True)
    grad_second = lax.dot_general(
        dbranch_full, activated, (((0,), (0,)), ((), ())), preferred_element_type=jnp.float32
    )
    dactivated = jnp.dot(dbranch_full, w_second, preferred_element_type=jnp.float32)
    dhidden = dactivated * slope
    grad_bin = jnp.sum(dhidden, 0)
    dhidden_low = dhidden.astype(jnp.bfloat16)
    grad_first = lax.dot_general(
        normed_full, dhidden_low, (((0,), (0,)), ((), ())), preferred_element_type=jnp.float32
    )
    dnormed_part = lax.dot_general(
        dhidden_low, w_first, (((1,), (1,)), ((), ())), preferred_element_type=jnp.float32
    )
    normalized_gradient = lax.psum_scatter(dnormed_part, "chan", scatter_dimension=1, tiled=True)
    norm_scale_gradient = jnp.sum(normalized_gradient * standardized_input, 0)
    grad_beta = jnp.sum(normalized_gradient, 0)
    standardized_gradient = normalized_gradient * norm_scale
    first_moment_sum, second_moment_sum = lax.psum(
        (jnp.sum(standardized_gradient, 1), jnp.sum(standardized_gradient * standardized_input, 1)),
        "chan",
    )
    first_moment = first_moment_sum / full_width
    second_moment = second_moment_sum / full_width
    convolution_gradient = (
        standardized_gradient - first_moment[:, None] - standardized_input * second_moment[:, None]
    ) * inverse_deviation[:, None]
    grad_dbias = jnp.sum(convolution_gradient, 0)
    grad_taps = kernel_grad(picked, convolution_gradient.reshape(picked.shape))
    grad_rows = jnp.concatenate(
        [
            grad_taps,
            grad_dbias[None],
            norm_scale_gradient[None],
            grad_beta[None],
            grad_bout[None],
            grad_scale[None],
        ],
        0,
    )
    return jnp.concatenate(
        [jnp.stack([grad_first, grad_second]).reshape(-1), grad_rows.reshape(-1), grad_bin]
    )


def flatten_state(matrices, channel_row_block, hidden_bias):
    return jnp.concatenate(
        [matrices.reshape(-1), channel_row_block.reshape(-1), hidden_bias.reshape(-1)]
    )


def unflatten_state(flattened, matrices, channel_row_block, hidden_bias):
    mats_size = matrices.size
    rows_size = channel_row_block.size
    return (
        flattened[:mats_size].reshape(matrices.shape),
        flattened[mats_size : mats_size + rows_size].reshape(channel_row_block.shape),
        flattened[mats_size + rows_size :].reshape(hidden_bias.shape),
    )


def on_device(
    images,
    cotangent,
    image_ids,
    counts,
    hop_exponents,
    param_mats,
    param_chans,
    param_bias,
    track_mats,
    track_chans,
    track_bias,
    grad_mats,
    grad_chans,
    grad_bias,
):
    layout = (param_mats.shape[1:], param_chans.shape[1:], param_bias.shape[1])
    params = flatten_state(param_mats, param_chans, param_bias)
    tracker = flatten_state(track_mats, track_chans, track_bias)
    previous = flatten_state(grad_mats, grad_chans, grad_bias)
    for iteration in range(ITERS):
        hop = hop_exponents[iteration]
        data_args = (
            images[iteration],
            cotangent[iteration, 0],
            image_ids[iteration, 0],
            counts[iteration, 0],
        )
        partner_state = swap_joint(jnp.stack([params, tracker]), hop)
        params = 0.5 * (params + partner_state[0]) - LEARNING_RATE * tracker
        fresh_grad = local_grad(params, layout, *data_args)
        tracker = 0.5 * (tracker + partner_state[1]) + fresh_grad - previous
        previous = fresh_grad
    out_params = unflatten_state(params, param_mats, param_chans, param_bias)
    out_tracker = unflatten_state(tracker, track_mats, track_chans, track_bias)
    return (
        out_params[0],
        out_params[1],
        out_params[2],
        out_tracker[0],
        out_tracker[1],
        out_tracker[2],
    )


def solution(mesh):
    in_specs = (
        P(None, "peer", None, None, "chan"),
        P(None, "peer", None, None, None, "chan"),
        P(None, "peer", None),
        P(None, "peer"),
        P(),
        P("peer", None, None, "chan"),
        P("peer", None, "chan"),
        P("peer", "chan"),
        P("peer", None, None, "chan"),
        P("peer", None, "chan"),
        P("peer", "chan"),
        P("peer", None, None, "chan"),
        P("peer", None, "chan"),
        P("peer", "chan"),
    )
    out_specs = (
        P("peer", None, None, "chan"),
        P("peer", None, "chan"),
        P("peer", "chan"),
        P("peer", None, None, "chan"),
        P("peer", None, "chan"),
        P("peer", "chan"),
    )
    return jax.shard_map(
        on_device, mesh=mesh, in_specs=in_specs, out_specs=out_specs, check_vma=False
    )
```

profile of v0, /device:TPU:1, one launch (start us, length us, event | category | flops | bytes accessed | tf_op | source)
XLA Modules:
  0.0 657.8 jit_solution(5404054952035961992)
XLA Ops:
  11.5 10.7 %stack.357 = f32[1,531712]{1,0:T(1,128)} reshape(f32[531712]{0:T(1024)S(1)} %pad_maximum_fusion.3) | data formatting | bytes 4253696 | tf_op jit(solution)/shard_map/stack | solution.py:219
  25.9 9.9 %stack.356 = f32[1,531712]{1,0:T(1,128)S(1)} reshape(f32[531712]{0:T(1024)S(1)} %pad_maximum_fusion.2) | data formatting | bytes 4253696 | tf_op jit(solution)/shard_map/stack | solution.py:219
  37.1 3.9 pad_maximum_fusion
  41.0 105.3 %conditional.2 = (f32[2,531712]{1,0:T(2,128)}) conditional(s32[]{:T(128)} %bitcast.1, f32[2,531712]{1,0:T(2,128)S(1)} %pad_maximum_fusion, f32[2,531712]{1,0:T(2,128)S(1)} %pad_maximum_fusion, f32[2,531712]{1,0:T(2,128)S(1)} %pad_maximum_fusion, f32[2,531712]{1,0:T(2,128)S(1)} %pad_maximum_fusion, ...), branch_computations={%region_0.1_spmd, %region_1.2_spmd, %region_2.3_spmd, %region_3.4_... | conditional | bytes 17014832 | solution.py:56
  41.1 2.5 collective-permute-start
  43.6 102.5 %collective-permute-done = f32[2,531712]{1,0:T(2,128)} collective-permute-done((f32[2,531712]{1,0:T(2,128)S(1)}, f32[2,531712]{1,0:T(2,128)}, u32[]{:S(2)}, u32[]{:S(2)}) %collective-permute-start) | collective-permute-done | bytes 4253728 | tf_op jit(solution)/shard_map/cond/branch_0_fun/ppermute | solution.py:15
  146.3 25.4 %slice_reduce_fusion.2 = (f32[531712]{0:T(1024)}, f32[531712]{0:T(1024)S(1)}) fusion(f32[2,531712]{1,0:T(2,128)} %get-tuple-element.296), kind=kLoop, calls=%fused_computation.140 | loop fusion | bytes 8507392 | tf_op jit(solution)/shard_map/slice | solution.py:222
  180.6 4.7 reshape.614
  185.3 2.5 convolution_convert_fusion.1
  188.0 3.7 fusion.228
  191.8 6.3 psum.56
  198.8 6.0 psum.57
  205.1 9.4 %all_gather.19 = bf16[784,512]{1,0:T(8,128)(2,1)S(1)} all-gather(bf16[784,128]{1,0:T(8,128)(2,1)S(1)} %add_convert_fusion.1), channel_id=1, replica_groups=mesh['peer'=32,'chan'=4] {'chan'}, dimensions={1}, use_global_device_ids=true | all-gather | bytes 1003520 | tf_op jit(solution)/shard_map/all_gather | solution.py:109
  215.4 3.0 multiply_convert_fusion.1
  227.9 19.0 %reduce-scatter.7.cloned.1.call-done = f32[784,128]{1,0:T(8,128)} async-done(((f32[784,512]{1,0:T(8,128)}), f32[784,128]{1,0:T(8,128)}) %reduce-scatter.7.cloned.1.call-update) | async-done | bytes 401424 | tf_op jit(solution)/shard_map/reduce_scatter | solution.py:119
  248.8 9.2 %all_gather.20 = bf16[784,512]{1,0:T(8,128)(2,1)S(1)} all-gather(bf16[784,128]{1,0:T(8,128)(2,1)S(1)} %get-tuple-element.271), channel_id=1, replica_groups=mesh['peer'=32,'chan'=4] {'chan'}, dimensions={1}, use_global_device_ids=true | all-gather | bytes 1003520 | tf_op jit(solution)/shard_map/all_gather | solution.py:130
  258.0 3.3 fusion.241
  264.1 5.2 copy.34
  269.3 3.5 copy.35
  272.8 3.5 copy.37
  281.8 43.0 %all-gather.7.cloned.1.call-done = bf16[32,2,25088]{2,1,0:T(2,128)(2,1)} async-done(((bf16[1,2,25088]{2,1,0:T(2,128)(2,1)}), bf16[32,2,25088]{2,1,0:T(2,128)(2,1)}) %all-gather.7.cloned.1.call-update) | async-done | bytes 3211280 | tf_op jit(solution)/shard_map/all_gather | solution.py:72
  324.8 4.9 reshape.616
  329.7 2.5 convolution_convert_fusion
  336.9 5.4 concatenate.66
  342.3 3.5 copy.38
  345.8 3.9 reduce-scatter.5.cloned.1.call-done
  351.3 5.5 all-reduce.3
  363.7 28.1 %fusion.2 = (f32[1,531712]{1,0:T(1,128)S(1)}, f32[1,531712]{1,0:T(1,128)S(1)}) fusion(f32[1,512]{1,0:T(1,128)S(1)} %copy-done.42, f32[1,6912]{1,0:T(1,128)S(1)} %bitcast.228, f32[1,524288]{1,0:T(1,128)} %bitcast.209, f32[2,531712]{1,0:T(2,128)} %get-tuple-element.296, f32[1,512]{1,0:T(1,128)S(1)} %copy-done.41, f32[1,6912]{1,0:T(1,128)S(1)} %bitcast.227, ...), kind=kLoop, calls=%fused_computation.114 | loop fusion | flops 8507392 | bytes 17014784 | tf_op jit(solution)/shard_map/sub | solution.py:220
  391.8 3.9 pad_maximum_fusion.1
  395.8 94.4 %conditional.3 = (f32[2,531712]{1,0:T(2,128)}) conditional(s32[]{:T(128)} %bitcast.3, f32[2,531712]{1,0:T(2,128)S(1)} %pad_maximum_fusion.1, f32[2,531712]{1,0:T(2,128)S(1)} %pad_maximum_fusion.1, f32[2,531712]{1,0:T(2,128)S(1)} %pad_maximum_fusion.1, f32[2,531712]{1,0:T(2,128)S(1)} %pad_maximum_fusion.1, ...), branch_computations={%region_70.71_spmd, %region_71.72_spmd, %region_72.73_spmd, %regio... | conditional | bytes 17014832 | solution.py:56
  395.8 3.0 collective-permute-start.6
  398.8 91.2 %collective-permute-done.6 = f32[2,531712]{1,0:T(2,128)} collective-permute-done((f32[2,531712]{1,0:T(2,128)S(1)}, f32[2,531712]{1,0:T(2,128)}, u32[]{:S(2)}, u32[]{:S(2)}) %collective-permute-start.6) | collective-permute-done | bytes 4253728 | tf_op jit(solution)/shard_map/cond/branch_1_fun/ppermute | solution.py:15
  490.3 25.4 %slice_reduce_fusion = (f32[531712]{0:T(1024)}, f32[531712]{0:T(1024)S(1)}) fusion(f32[2,531712]{1,0:T(2,128)} %get-tuple-element.297), kind=kLoop, calls=%fused_computation.110 | loop fusion | bytes 8507392 | tf_op jit(solution)/shard_map/slice | solution.py:222
  515.7 3.7 fusion.224
  520.7 3.6 fusion.225
  524.4 6.8 %psum.60 = f32[784]{0:T(1024)S(1)} all-reduce(f32[784]{0:T(1024)S(1)} %reduce_sum.1132), channel_id=1, replica_groups=mesh['peer'=32,'chan'=4] {'chan'}, use_global_device_ids=true, to_apply=%region_76.77 | all-reduce | flops 784 | bytes 6272 | tf_op jit(solution)/shard_map/psum | solution.py:100
  531.8 5.8 psum.61
  538.0 9.6 %all_gather.22 = bf16[784,512]{1,0:T(8,128)(2,1)} all-gather(bf16[784,128]{1,0:T(8,128)(2,1)S(1)} %add_convert_fusion), channel_id=1, replica_groups=mesh['peer'=32,'chan'=4] {'chan'}, dimensions={1}, use_global_device_ids=true | all-gather | bytes 1003520 | tf_op jit(solution)/shard_map/all_gather | solution.py:109
  552.1 3.1 multiply_convert_fusion
  563.1 20.1 %reduce-scatter.11.cloned.1.call-done = f32[784,128]{1,0:T(8,128)} async-done(((f32[784,512]{1,0:T(8,128)}), f32[784,128]{1,0:T(8,128)}) %reduce-scatter.11.cloned.1.call-update) | async-done | bytes 401424 | tf_op jit(solution)/shard_map/reduce_scatter | solution.py:119
  585.0 9.1 %all_gather.23 = bf16[784,512]{1,0:T(8,128)(2,1)S(1)} all-gather(bf16[784,128]{1,0:T(8,128)(2,1)S(1)} %get-tuple-element.269), channel_id=1, replica_groups=mesh['peer'=32,'chan'=4] {'chan'}, dimensions={1}, use_global_device_ids=true | all-gather | bytes 1003520 | tf_op jit(solution)/shard_map/all_gather | solution.py:130
  594.1 2.9 fusion.242
  600.6 3.0 slice.1323
  604.4 2.8 reshape.598
  613.4 11.5 %reduce-scatter.9.cloned.1.call-done = f32[784,128]{1,0:T(8,128)} async-done(((f32[784,512]{1,0:T(8,128)}), f32[784,128]{1,0:T(8,128)}) %reduce-scatter.9.cloned.1.call-update) | async-done | bytes 401424 | tf_op jit(solution)/shard_map/reduce_scatter | solution.py:144
  626.4 5.5 all-reduce.2
  638.7 5.9 fusion
  647.2 2.7 reshape.606
  (225 shorter events, 88.9 us)
Async XLA Ops:
  7.2 173.4 %all-gather.5.cloned.1.call-start = ((), (), s32[]{:S(2)}) async-start(), calls=%async_computation.8 | async-start | bytes 3311616 | tf_op jit(solution)/shard_map/all_gather | solution.py:72
  9.0 238.0 %reduce-scatter.7.cloned.1.call-start = ((), (), s32[]{:S(2)}) async-start(), calls=%async_computation.5 | async-start | bytes 2007040 | tf_op jit(solution)/shard_map/reduce_scatter | solution.py:119
  11.3 160.4 %copy-start.30 = (f32[54,128]{1,0:T(8,128)}, f32[54,128]{1,0:T(8,128)S(1)}, u32[]{:S(2)}) copy-start(f32[54,128]{1,0:T(8,128)S(1)} %reduce.9) | copy-start | bytes 82948
  11.4 10.7 %copy-start.9 = (f32[1,2,512,512]{3,2,1,0:T(8,128)S(1)}, f32[1,2,512,512]{3,2,1,0:T(8,128)}, u32[]{:S(2)}) copy-start(f32[1,2,512,512]{3,2,1,0:T(8,128)} %param.29) | copy-start | bytes 6291460
  25.9 10.0 %copy-start.53 = (s32[2]{0:T(128)S(1)}, s32[2]{0:T(128)}, u32[]{:S(2)}) copy-start(s32[2]{0:T(128)} %param.28) | copy-start | bytes 28
  25.9 11.2 %copy-start.8 = (f32[1,531712]{1,0:T(1,128)S(1)}, f32[1,531712]{1,0:T(1,128)}, u32[]{:S(2)}) copy-start(f32[1,531712]{1,0:T(1,128)} %stack.357) | copy-start | bytes 6380548
  41.1 105.1 %collective-permute-start = (f32[2,531712]{1,0:T(2,128)S(1)}, f32[2,531712]{1,0:T(2,128)}, u32[]{:S(2)}, u32[]{:S(2)}) collective-permute-start(f32[2,531712]{1,0:T(2,128)S(1)} %param), channel_id=1, source_target_pairs={{0,4},{4,0},{8,12},{12,8},{16,20},{20,16},{24,28},{28,24},{32,36},... | collective-permute-start | bytes 12761096 | tf_op jit(solution)/shard_map/cond/branch_0_fun/ppermute | solution.py:15
  146.3 25.4 %copy-start.1 = (f32[128,4,8,128]{3,1,2,0:T(4,128)S(1)}, f32[128,4,8,128]{3,1,2,0:T(4,128)}, u32[]{:S(2)}) copy-start(f32[128,4,8,128]{3,1,2,0:T(4,128)} %copy.32) | copy-start | bytes 6291460
  172.1 4.2 copy-start.54
  172.1 5.4 copy-start.55
  179.5 25.3 %copy-start.47 = (f32[128]{0:T(128)}, f32[128]{0:T(128)S(1)}, u32[]{:S(2)}) copy-start(f32[128]{0:T(128)S(1)} %get-tuple-element.213) | copy-start | bytes 1540
  215.4 3.9 copy-start.14
  221.1 103.8 %all-gather.7.cloned.1.call-start = ((), (), s32[]{:S(2)}) async-start(), calls=%async_computation.9 | async-start | bytes 3311616 | tf_op jit(solution)/shard_map/all_gather | solution.py:72
  221.8 127.9 %reduce-scatter.5.cloned.1.call-start = ((), (), s32[]{:S(2)}) async-start(), calls=%async_computation.4 | async-start | bytes 2007040 | tf_op jit(solution)/shard_map/reduce_scatter | solution.py:144
  258.0 3.3 copy-start.24
  258.0 4.3 copy-start.13
  264.1 319.1 %reduce-scatter.11.cloned.1.call-start = ((), (), s32[]{:S(2)}) async-start(), calls=%async_computation.7 | async-start | bytes 2007040 | tf_op jit(solution)/shard_map/reduce_scatter | solution.py:119
  264.1 5.2 copy-start.10
  269.3 3.5 copy-start.11
  277.0 3.2 copy-start.16
  342.3 7.4 %copy-start.48 = (f32[128]{0:T(128)S(1)}, f32[128]{0:T(128)}, u32[]{:S(2)}) copy-start(f32[128]{0:T(128)} %copy-done.47) | copy-start | bytes 1540
  356.8 6.7 %copy-start.49 = (f32[128]{0:T(128)S(1)}, f32[128]{0:T(128)}, u32[]{:S(2)}) copy-start(f32[128]{0:T(128)} %get-tuple-element.270) | copy-start | bytes 1540
  356.8 6.7 %copy-start.51 = (f32[128]{0:T(128)S(1)}, f32[128]{0:T(128)}, u32[]{:S(2)}) copy-start(f32[128]{0:T(128)} %multiply_reduce_fusion.8) | copy-start | bytes 1540
  356.8 6.9 %copy-start.38 = (f32[1,54,128]{2,0,1:T(1,128)S(1)}, f32[1,54,128]{2,0,1:T(1,128)}, u32[]{:S(2)}) copy-start(f32[1,54,128]{2,0,1:T(1,128)} %param.33) | copy-start | bytes 82948
  356.8 6.9 %copy-start.40 = (f32[1,54,128]{2,0,1:T(1,128)S(1)}, f32[1,54,128]{2,0,1:T(1,128)}, u32[]{:S(2)}) copy-start(f32[1,54,128]{2,0,1:T(1,128)} %param.30) | copy-start | bytes 82948
  356.8 6.9 %copy-start.43 = (f32[1,512]{1,0:T(1,128)S(1)}, f32[1,512]{1,0:T(1,128)}, u32[]{:S(2)}) copy-start(f32[1,512]{1,0:T(1,128)} %param.37) | copy-start | bytes 6148
  356.8 6.9 %copy-start.45 = (f32[512]{0:T(512)S(1)}, f32[512]{0:T(512)}, u32[]{:S(2)}) copy-start(f32[512]{0:T(512)} %get-tuple-element.284) | copy-start | bytes 6148
  363.7 152.0 %copy-start.32 = (f32[54,128]{1,0:T(8,128)}, f32[54,128]{1,0:T(8,128)S(1)}, u32[]{:S(2)}) copy-start(f32[54,128]{1,0:T(8,128)S(1)} %concatenate.67) | copy-start | bytes 82948
  395.8 94.2 %collective-permute-start.6 = (f32[2,531712]{1,0:T(2,128)S(1)}, f32[2,531712]{1,0:T(2,128)}, u32[]{:S(2)}, u32[]{:S(2)}) collective-permute-start(f32[2,531712]{1,0:T(2,128)S(1)} %param.6), channel_id=1, source_target_pairs={{0,8},{4,12},{8,0},{12,4},{16,24},{20,28},{24,16},{28,20},{32,40},... | collective-permute-start | bytes 12761096 | tf_op jit(solution)/shard_map/cond/branch_1_fun/ppermute | solution.py:15
  490.2 25.4 %copy-start = (f32[531712]{0:T(1024)S(1)}, f32[531712]{0:T(1024)}, u32[]{:S(2)}) copy-start(f32[531712]{0:T(1024)} %get-tuple-element.30) | copy-start | bytes 6380548
  490.2 25.4 %copy-start.2 = (f32[128,4,8,128]{3,1,2,0:T(4,128)S(1)}, f32[128,4,8,128]{3,1,2,0:T(4,128)}, u32[]{:S(2)}) copy-start(f32[128,4,8,128]{3,1,2,0:T(4,128)} %copy.39) | copy-start | bytes 6291460
  490.2 25.4 %copy-start.3 = (f32[128,4,8,128]{3,1,2,0:T(4,128)S(1)}, f32[128,4,8,128]{3,1,2,0:T(4,128)}, u32[]{:S(2)}) copy-start(f32[128,4,8,128]{3,1,2,0:T(4,128)} %copy.38) | copy-start | bytes 6291460
  490.2 25.4 %copy-start.5 = (f32[531712]{0:T(1024)S(1)}, f32[531712]{0:T(1024)}, u32[]{:S(2)}) copy-start(f32[531712]{0:T(1024)} %copy-done.4) | copy-start | bytes 6380548
  490.2 25.4 %copy-start.31 = (f32[54,128]{1,0:T(8,128)S(1)}, f32[54,128]{1,0:T(8,128)}, u32[]{:S(2)}) copy-start(f32[54,128]{1,0:T(8,128)} %copy-done.30) | copy-start | bytes 82948
  490.2 25.4 %copy-start.34 = (f32[54,128]{1,0:T(8,128)S(1)}, f32[54,128]{1,0:T(8,128)}, u32[]{:S(2)}) copy-start(f32[54,128]{1,0:T(8,128)} %reduce.13) | copy-start | bytes 82948
  520.7 31.5 %copy-start.52 = (f32[512]{0:T(512)}, f32[512]{0:T(512)S(1)}, u32[]{:S(2)}) copy-start(f32[512]{0:T(512)S(1)} %slice.1325) | copy-start | bytes 6148
  537.7 9.9 %copy-start.12 = (bf16[531712]{0:T(1024)(128)(2,1)S(1)}, bf16[531712]{0:T(1024)(128)(2,1)}, u32[]{:S(2)}) copy-start(bf16[531712]{0:T(1024)(128)(2,1)} %get-tuple-element.145) | copy-start | bytes 3190276
  552.1 3.9 copy-start.15
  557.9 67.0 %reduce-scatter.9.cloned.1.call-start = ((), (), s32[]{:S(2)}) async-start(), calls=%async_computation.6 | async-start | bytes 2007040 | tf_op jit(solution)/shard_map/reduce_scatter | solution.py:144
  594.1 2.9 copy-start.27
  604.4 3.4 copy-start.17
  607.8 2.8 copy-start.28
  611.5 20.4 %copy-start.18 = (f32[784,128]{1,0:T(8,128)S(1)}, f32[784,128]{1,0:T(8,128)}, u32[]{:S(2)}) copy-start(f32[784,128]{1,0:T(8,128)} %reshape.612) | copy-start | bytes 1204228
  631.9 6.6 %copy-start.50 = (f32[128]{0:T(128)S(1)}, f32[128]{0:T(128)}, u32[]{:S(2)}) copy-start(f32[128]{0:T(128)} %get-tuple-element.268) | copy-start | bytes 1540
  631.9 6.8 %copy-start.33 = (f32[54,128]{1,0:T(8,128)S(1)}, f32[54,128]{1,0:T(8,128)}, u32[]{:S(2)}) copy-start(f32[54,128]{1,0:T(8,128)} %copy-done.32) | copy-start | bytes 82948
  631.9 6.8 %copy-start.35 = (f32[54,128]{1,0:T(8,128)S(1)}, f32[54,128]{1,0:T(8,128)}, u32[]{:S(2)}) copy-start(f32[54,128]{1,0:T(8,128)} %reduce.13) | copy-start | bytes 82948
  631.9 6.8 %copy-start.44 = (f32[1,512]{1,0:T(1,128)S(1)}, f32[1,512]{1,0:T(1,128)}, u32[]{:S(2)}) copy-start(f32[1,512]{1,0:T(1,128)} %param.37) | copy-start | bytes 6148
  631.9 6.8 %copy-start.46 = (f32[512]{0:T(512)S(1)}, f32[512]{0:T(512)}, u32[]{:S(2)}) copy-start(f32[512]{0:T(512)} %get-tuple-element.284) | copy-start | bytes 6148
  (17 other events, 30.0 us)
Sparse Core Ops, SparseCore 0:
  11.0 79.5 all-gather.4
  221.2 25.7 reduce-scatter.6
  249.9 74.8 all-gather.6
  327.1 22.5 reduce-scatter.4
  558.0 25.1 reduce-scatter.10
  599.9 24.9 reduce-scatter.8
where the time goes:
time: 662 us; the launch traced here: 658 us
  waiting for transfers between devices  292 us (44%)
  local copies, waits for them, and re-layouts  156 us (24%)
  other arithmetic  82.2 us (12%)
  blocking collectives  73.1 us (11%)
  matrix products  30.5 us (5%)
  between operations  18.2 us (3%)
    ppermute x2, waiting for transfers between devices, partner(): lax.ppermute(value, axis, [(i, i ^ 1 << stride) for i in range(lax.axis_s...  194 us
    slice x2, local copies, waits for them, and re-layouts, on_device(): tracker = 0.5 * (tracker + partner_state[1]) + fresh_grad - previous  50.7 us
    all_gather x2, waiting for transfers between devices, fetch_images(): piece = lax.all_gather(flat_images, 'peer', axis=0, tiled=True)  43 us
    unnamed x123, local copies, waits for them, and re-layouts  40.8 us
    reduce_scatter x2, waiting for transfers between devices, local_grad(): lax.psum_scatter(partial_out, 'chan', scatter_dimension=1, tiled=True)  39.2 us
    sub x1, other arithmetic, on_device(): params = 0.5 * (params + partner_state[0]) - LEARNING_RATE * tracker  28.1 us
    another operation x2, local copies, waits for them, and re-layouts, on_device(): partner_state = swap_joint(jnp.stack([params, tracker]), hop)  20.6 us
    all_gather x2, blocking collectives, local_grad(): normed_full = lax.all_gather(normalized_rows, 'chan', axis=1, tiled=True)  19 us
  transfers between devices with their start and end apart: 8, of which 7 were waited for; matrix products, arithmetic and copies ran while one was open for 20% of the time, Pallas kernels for 0%

commit v1 on v0

v1 whole, which is shorter than its diff:
```python
import functools

import jax
import jax.numpy as jnp
from jax import lax
from jax.experimental import pallas as pl
from jax.experimental.pallas import tpu as pltpu
from jax.sharding import PartitionSpec as P

KS = 7
TAPS = KS * KS
ITERS = 2
EPS = 1e-06
LEARNING_RATE = 0.01
MESH = pl.DeviceIdType.MESH
F32 = jnp.float32
BF16 = jnp.bfloat16
HIGHEST = lax.Precision.HIGHEST

SIDE = 14
PADW = 16
SLOTS = 4
SROWS = SIDE * PADW
ROWS = SLOTS * SROWS
CW = 128
C = 512
HID = 512
NCHUNK = 8
CROWS = 128
NCHAN = 4
STATW = ROWS + CW


def aligned(value, step):
    return pl.multiple_of(value, step)


def dot(a, b, ca, cb, precision=None):
    return lax.dot_general(
        a, b, (((ca,), (cb,)), ((), ())), precision=precision, preferred_element_type=F32
    )


def lane_sums(values):
    return dot(jnp.ones((8, CW), F32), values, 1, 1, HIGHEST)


def two_rows(first, second):
    row = lax.broadcasted_iota(jnp.int32, (8, first.shape[-1]), 0)
    return jnp.where(row == 0, first, jnp.where(row == 1, second, 0.0))


def two_columns(rows):
    row = lax.broadcasted_iota(jnp.int32, (8, 2 * CW), 0)
    lane = lax.broadcasted_iota(jnp.int32, (8, 2 * CW), 1)
    pick = jnp.where((lane < CW) & (row == 0), 1.0, 0.0) + jnp.where(
        (lane >= CW) & (row == 1), 1.0, 0.0
    )
    both = dot(rows, pick, 0, 0, HIGHEST)
    return both[:, :CW], both[:, CW:]


def kernel(t, hop, names, *refs):
    r = dict(zip(names, refs))
    first = t == 0
    peer = lax.axis_index("peer")
    chan = lax.axis_index("chan")
    my_z, my_y, my_x = peer % 4, (peer // 4) % 2, peer // 8
    core, side = chan % 2, chan // 2

    def at(new_peer, new_chan):
        return (new_peer, new_chan)

    c_core = side * 2 + 1 - core
    c_side = (1 - side) * 2 + core
    c_diag = (1 - side) * 2 + 1 - core
    d_core, d_side, d_diag = at(peer, c_core), at(peer, c_side), at(peer, c_diag)
    bit = (peer // (2**hop)) % 2
    d_hop = at(peer + (1 - 2 * bit) * (2**hop), chan)
    d_yhi = at(peer + (1 - 2 * my_y) * 4, chan)
    zs = [(my_z + d) % 4 for d in (1, 2, 3)]
    xs = [(my_x + d) % 4 for d in (1, 2, 3)]
    d_zs = [at(peer - my_z + z, chan) for z in zs]
    d_xs = [at(peer + (x - my_x) * 8, chan) for x in xs]

    counters = {"remote": 0, "local": 0}
    ends = []

    def take(kind, n):
        start = counters[kind]
        counters[kind] += n
        return start

    def remote(src, dst, device, index):
        return pltpu.make_async_remote_copy(
            src_ref=src,
            dst_ref=dst,
            send_sem=r["send"].at[index],
            recv_sem=r["recv"].at[index],
            device_id=device,
            device_id_type=MESH,
        )

    def push(src, dst, device):
        copy = remote(src, dst, device, take("remote", 1))
        copy.start()
        ends.append(copy.wait_send)
        return copy

    def local(src, dst):
        copy = pltpu.make_async_copy(src, dst, r["local"].at[take("local", 1)])
        copy.start()
        return copy

    P2, Y2, G2, F2 = r["P2"], r["Y2"], r["G2"], r["F2"]
    PB, PP, YB, YP, W = r["PB"], r["PP"], r["YB"], r["YP"], r["W"]

    def piece(ref, i):
        return ref.at[i // 4, pl.ds(aligned((i % 4) * CROWS, CROWS), CROWS), :]

    if first:
        G = [r["G0"], r["G1"]]
        own_rows = my_z * 4 + my_y * 2
        img_in = [local(r["images"].at[u], G[u].at[pl.ds(own_rows, 2)]) for u in range(2)]
    p_sem = take("local", NCHUNK)

    def p_load(i):
        return pltpu.make_async_copy(
            piece(r["pm"].at[0], i), piece(P2, i), r["local"].at[p_sem + i]
        )

    def start_p(i, carry):
        p_load(i).start()
        return carry

    lax.fori_loop(0, NCHUNK, start_p, 0)
    cot_in = local(r["cot"].at[t, 0], r["COTL"])
    y_in = local(r["ym"].at[0], Y2)
    g_in = local(r["gm"].at[0], G2)

    count = r["counts"][t, 0]

    def valid(s):
        return jnp.where(s < count, 1.0, 0.0).astype(F32)

    inv = 1.0 / jnp.full((1, CW), count.astype(F32))

    if first:
        IDV = r["IDV"]
        lane = lax.broadcasted_iota(jnp.int32, (8, 128), 1)
        row = lax.broadcasted_iota(jnp.int32, (8, 128), 0)
        tile = jnp.zeros((8, 128), jnp.int32)
        for u in range(2):
            for s in range(SLOTS):
                tile = jnp.where((row == u) & (lane == s), r["ids"][u, 0, s], tile)
        IDV[my_x] = tile

    barrier = pltpu.get_barrier_semaphore()
    greet = [d_core, d_side, d_diag] + ([d_yhi] + d_zs + d_xs if first else [d_hop])
    for device in greet:
        pl.semaphore_signal(barrier, inc=1, device_id=device, device_id_type=MESH)
    pl.semaphore_wait(barrier, len(greet))

    small = [
        push(r["pc"].at[0], r["RPC"], d_hop),
        push(r["pb"], r["RPB"], d_hop),
        push(r["yc"].at[0], r["RYC"], d_hop),
        push(r["yb"], r["RYB"], d_hop),
    ]

    fetch = {}
    if first:
        fetch["ids"] = [push(IDV.at[my_x], IDV.at[my_x], d) for d in d_xs]

    def images_begin(u):
        img_in[u].wait()
        mine = G[u].at[pl.ds(own_rows, 2)]
        fetch["y", u] = push(mine, mine, d_yhi)
        fetch["za", u] = [push(mine, mine, d) for d in d_zs]

    def images_second(u):
        fetch["y", u].wait_recv()
        other = G[u].at[pl.ds(my_z * 4 + (1 - my_y) * 2, 2)]
        fetch["zb", u] = [push(other, other, d) for d in d_zs]

    def wanted_row(source, u, s):
        ident = r["IDS"][source, u, s]
        return ((ident // 2) % 4) * 4 + ((ident // 8) % 2) * 2 + ident % 2

    def images_third(u):
        for copy in fetch["za", u] + fetch["zb", u]:
            copy.wait_recv()
        XS, XR = r["XS"], r["XR%d" % u]
        for j in range(3):
            for s in range(SLOTS):
                XS[u, j, s] = G[u][wanted_row(xs[j], u, s)]
        fetch["x", u] = [push(XS.at[u, j], XR.at[my_x], d_xs[j]) for j in range(3)]
        for s in range(SLOTS):
            XR[my_x, s] = G[u][wanted_row(my_x, u, s)]

    def images_end(u):
        for copy in fetch["x", u]:
            copy.wait_recv()

    def picked(u, s):
        return r["XR%d" % u][(r["IDS"][my_x, u, s] // 16) % 4, s]

    if first:
        images_begin(0)

    p_send = take("remote", NCHUNK)

    def p_copy(i):
        return remote(piece(PB, i), piece(PP, i), d_hop, p_send + i)

    def rows_of(i):
        return (i // 4, pl.ds(aligned((i % 4) * CROWS, CROWS), CROWS), slice(None))

    def send_p(i, carry):
        p_load(i).wait()
        PB[rows_of(i)] = P2[rows_of(i)].astype(BF16)
        p_copy(i).start()
        return carry

    lax.fori_loop(0, NCHUNK, send_p, 0)

    CF, CP = r["CF"], r["CP"]
    my_lanes = pl.ds(aligned(chan * CW, CW), CW)
    side_lanes = pl.ds(aligned(c_side * CW, CW), CW)
    CP[...] = jnp.zeros_like(CP)
    r["XP"][...] = jnp.zeros_like(r["XP"])
    cot_in.wait()
    cot_sum = jnp.zeros((1, CW), F32)
    for s in range(SLOTS):
        CP[s, :, 0:SIDE, :] = r["COTL"][s].astype(F32) * valid(s)
        flat = CP[s].reshape(SROWS, CW)
        cot_sum = cot_sum + jnp.sum(flat, 0, keepdims=True)
        CF[s * SROWS : (s + 1) * SROWS, my_lanes] = flat.astype(BF16)
    cot_core = push(CF.at[:, my_lanes], CF.at[:, my_lanes], d_core)
    cot_side = push(CF.at[:, my_lanes], CF.at[:, my_lanes], d_side)

    for copy in small:
        copy.wait_recv()
    qc, qb = r["qc"], r["qb"]
    qc[0] = 0.5 * (r["pc"][0] + r["RPC"][...]) - LEARNING_RATE * r["yc"][0]
    qb[...] = 0.5 * (r["pb"][...] + r["RPB"][...]) - LEARNING_RATE * r["yb"][...]

    def chan_row(k):
        return qc[0, k : k + 1, :]

    if first:
        images_second(0)
        for copy in fetch["ids"]:
            copy.wait_recv()
        ids_in = local(IDV, r["IDS"])
        ids_in.wait()
        images_third(0)
        images_begin(1)
        images_end(0)

    XP, SH, X = r["XP"], r["SH"], r["X"]
    for s in range(SLOTS):
        image = picked(0, s) if first else r["picked"][s]
        XP[s, 3 : 3 + SIDE, 3 : 3 + SIDE, :] = image.astype(F32) * valid(s)

    def shift(s, carry):
        for v in range(KS):
            SH[v, s] = XP[s, :, v : v + PADW, :]
        return carry

    lax.fori_loop(0, SLOTS, shift, 0)

    def conv_slot(s, carry):
        def column(v, acc):
            for u in range(KS):
                acc = acc + SH[v, s, u : u + SIDE] * qc[0, pl.ds(u * KS + v, 1), :]
            return acc

        acc = lax.fori_loop(0, KS, column, jnp.zeros((SIDE, PADW, CW), F32))
        X[pl.ds(aligned(s * SROWS, SROWS), SROWS), :] = acc.reshape(SROWS, CW) + chan_row(TAPS)
        return carry

    lax.fori_loop(0, SLOTS, conv_slot, 0)

    STR = r["STR"]
    conv_out = X[...]
    mean_here = jnp.sum(conv_out, 1, keepdims=True) * (1.0 / CW)
    centred = conv_out - mean_here
    mean_row = dot(jnp.full((8, CW), 1.0 / CW, F32), conv_out, 1, 1, HIGHEST)
    STR[chan, :, 0:ROWS] = two_rows(mean_row, lane_sums(centred * centred))
    STR[chan, :, ROWS:STATW] = jnp.broadcast_to(chan_row(TAPS + 4), (8, CW))
    stats = [push(STR.at[chan], STR.at[chan], d) for d in (d_core, d_side, d_diag)]
    cot_side.wait_recv()
    cot_far = push(CF.at[:, side_lanes], CF.at[:, side_lanes], d_core)
    for copy in stats:
        copy.wait_recv()
    means = [STR[j, 0:1, 0:ROWS] for j in range(NCHAN)]
    mean = (means[0] + means[1] + means[2] + means[3]) * 0.25
    squares = STR[0, 1:2, 0:ROWS] + STR[1, 1:2, 0:ROWS] + STR[2, 1:2, 0:ROWS] + STR[3, 1:2, 0:ROWS]
    for j in range(NCHAN):
        squares = squares + CW * (means[j] - mean) * (means[j] - mean)
    deviation = lax.rsqrt(squares * (1.0 / C) + EPS)
    mean_col, inv_col = two_columns(two_rows(mean, deviation))
    r["INV"][...] = inv_col
    xhat = (X[...] - mean_col) * inv_col
    X[...] = xhat
    NF = r["NF"]
    NF[:, my_lanes] = (xhat * chan_row(TAPS + 1) + chan_row(TAPS + 2)).astype(BF16)

    na, nb, nc = take("remote", SLOTS), take("remote", SLOTS), take("remote", SLOTS)

    def slot_rows(s):
        return pl.ds(aligned(s * SROWS, SROWS), SROWS)

    def norm_core(s):
        part = NF.at[slot_rows(s), my_lanes]
        return remote(part, part, d_core, na + s)

    def norm_side(s):
        part = NF.at[slot_rows(s), my_lanes]
        return remote(part, part, d_side, nb + s)

    def norm_far(s):
        part = NF.at[slot_rows(s), side_lanes]
        return remote(part, part, d_core, nc + s)

    def norm_send(s, carry):
        norm_side(s).start()
        norm_core(s).start()
        return carry

    lax.fori_loop(0, SLOTS, norm_send, 0)

    cot_core.wait_recv()
    cot_far.wait_recv()
    DB = r["DB"]
    for j in range(NCHAN):
        lanes = slice(j * CW, (j + 1) * CW)
        factor = inv * STR[j, 0:1, ROWS:STATW]
        DB[:, lanes] = (CF[:, lanes].astype(F32) * factor).astype(BF16)

    y_in.wait()

    def mix(i, carry):
        p_copy(i).wait_recv()
        q = 0.5 * (P2[rows_of(i)] + PP[rows_of(i)].astype(F32)) - LEARNING_RATE * Y2[rows_of(i)]
        P2[rows_of(i)] = q
        W[rows_of(i)] = q.astype(BF16)
        return carry

    lax.fori_loop(0, NCHUNK, mix, 0)
    q_out = local(P2, r["qm"].at[0])

    y_send = take("remote", NCHUNK)

    def y_copy(i):
        return remote(piece(YB, i), piece(YP, i), d_hop, y_send + i)

    def send_y(i, carry):
        YB[rows_of(i)] = Y2[rows_of(i)].astype(BF16)
        y_copy(i).start()
        return carry

    lax.fori_loop(0, NCHUNK, send_y, 0)

    ACT, DH, DP, R1, S2, R2, DN = (r[n] for n in ("ACT", "DH", "DP", "R1", "S2", "R2", "DN"))
    r1, r2 = take("remote", 2 * SLOTS), take("remote", SLOTS)

    def near_copy(s, b):
        lanes = pl.ds(aligned((b * 2 + 1 - core) * CW, CW), CW)
        return remote(DP.at[slot_rows(s), lanes], R1.at[b, slot_rows(s)], d_core, r1 + 2 * s + b)

    def far_copy(s):
        return remote(S2.at[slot_rows(s)], R2.at[slot_rows(s)], d_side, r2 + s)

    GB = r["GB"]
    GB[...] = jnp.zeros_like(GB)

    def slot_step(step, carry):
        @pl.when(step < SLOTS)
        def _():
            norm_side(step).wait_recv()
            norm_far(step).start()

        @pl.when((step > 0) & (step <= SLOTS))
        def _():
            s = step - 1
            norm_core(s).wait_recv()
            norm_far(s).wait_recv()
            rows = slot_rows(s)
            hidden = dot(NF[rows, :], W[0], 1, 0) + qb[...]
            cdf = 0.5 * (1.0 + lax.erf(hidden * 0.7071067811865476))
            density = jnp.exp(-0.5 * hidden * hidden) * 0.3989422804014327
            ACT[rows, :] = (hidden * cdf).astype(BF16)
            slope = cdf + hidden * density
            dhidden = dot(DB[rows, :], W[1], 1, 0) * slope
            GB[...] += jnp.sum(dhidden, 0, keepdims=True)
            low = dhidden.astype(BF16)
            DH[rows, :] = low
            DP[rows, :] = dot(low, W[0], 1, 1)
            near_copy(s, 0).start()
            near_copy(s, 1).start()

        @pl.when(step > 1)
        def _():
            s = step - 2
            rows = slot_rows(s)
            near_copy(s, 0).wait_recv()
            near_copy(s, 1).wait_recv()
            S2[rows, :] = (DP[rows, side_lanes] + R1[1 - side, rows, :]).astype(BF16)
            far_copy(s).start()
            DN[rows, :] = DP[rows, my_lanes] + R1[side, rows, :]

        return carry

    lax.fori_loop(0, SLOTS + 2, slot_step, 0)

    if first:
        images_second(1)

    BS, BR, GS = r["BS"], r["BR"], r["GS"]

    def scale_part(j, carry):
        lanes = pl.ds(aligned(j * CW, CW), CW)
        rows = pl.ds(aligned(j * CW, CW), CW)
        pair = dot(CF[:, lanes], ACT[...], 0, 0)
        weight = W[1, rows, :].astype(F32)
        GS[j] = dot(jnp.ones((8, HID), F32), pair * weight, 1, 1, HIGHEST)
        return carry

    lax.fori_loop(0, NCHAN, scale_part, 0)

    def far_wait(s, carry):
        far_copy(s).wait_recv()
        return carry

    lax.fori_loop(0, SLOTS, far_wait, 0)
    dnormed = DN[...] + R2[...].astype(F32)
    DN[...] = dnormed
    xhat = X[...]
    dxhat = dnormed * chan_row(TAPS + 1)
    sums = two_rows(lane_sums(dxhat), lane_sums(dxhat * xhat))
    for j in range(NCHAN):
        BS[j, :, 0:ROWS] = sums
        BS[j, :, ROWS:STATW] = GS[j]
    BR[chan] = BS[chan]
    back = [
        push(BS.at[c], BR.at[chan], d)
        for c, d in ((c_core, d_core), (c_side, d_side), (c_diag, d_diag))
    ]

    def mats_part(j, carry):
        lanes = pl.ds(aligned(j * CW, CW), CW)
        F2[0, lanes, :] = dot(NF[:, lanes], DH[...], 0, 0)
        F2[1, lanes, :] = dot(DB[:, lanes], ACT[...], 0, 0)
        return carry

    lax.fori_loop(0, NCHAN, mats_part, 0)
    if first:
        f_out = local(F2, r["fm"].at[0])

    if first:
        images_third(1)

    for copy in back:
        copy.wait_recv()
    totals = BR[0] + BR[1] + BR[2] + BR[3]
    mean_a, mean_b = two_columns(totals[:, 0:ROWS] * (1.0 / C))
    dnormed = DN[...]
    xhat = X[...]
    dconv = (dnormed * chan_row(TAPS + 1) - mean_a - xhat * mean_b) * r["INV"][...]
    DC, FC = r["DC"], r["FC"]
    DC[...] = dconv.reshape(SLOTS, SIDE, PADW, CW)
    FC[TAPS : TAPS + 1, :] = jnp.sum(dconv, 0, keepdims=True)
    FC[TAPS + 1 : TAPS + 2, :] = jnp.sum(dnormed * xhat, 0, keepdims=True)
    FC[TAPS + 2 : TAPS + 3, :] = jnp.sum(dnormed, 0, keepdims=True)
    FC[TAPS + 3 : TAPS + 4, :] = chan_row(TAPS + 4) * inv * cot_sum
    FC[TAPS + 4 : TAPS + 5, :] = inv * (totals[0:1, ROWS:STATW] + chan_row(TAPS + 3) * cot_sum)

    def tap_column(v, carry):
        def over(s, accs):
            grad = DC[s]
            return tuple(
                accs[u] + jnp.sum(SH[v, s, u : u + SIDE] * grad, 0) for u in range(KS)
            )

        accs = lax.fori_loop(0, SLOTS, over, tuple(jnp.zeros((PADW, CW), F32) for _ in range(KS)))
        for u in range(KS):
            FC[pl.ds(u * KS + v, 1), :] = jnp.sum(accs[u], 0, keepdims=True)
        return carry

    lax.fori_loop(0, KS, tap_column, 0)

    fresh = FC[0 : TAPS + 5, :]
    r["new_yc"][0] = 0.5 * (r["yc"][0] + r["RYC"][...]) + fresh - r["gc"][0]
    r["new_yb"][...] = 0.5 * (r["yb"][...] + r["RYB"][...]) + GB[...] - r["gb"][...]
    if first:
        r["fc"][0] = fresh
        r["fb"][...] = GB[...]
        images_end(1)
        for s in range(SLOTS):
            r["picked_next"][s] = picked(1, s)

    g_in.wait()
    out_sem = take("local", NCHUNK)

    def y_out(i):
        return pltpu.make_async_copy(
            piece(Y2, i), piece(r["new_ym"].at[0], i), r["local"].at[out_sem + i]
        )

    def track(i, carry):
        y_copy(i).wait_recv()
        at_i = rows_of(i)
        Y2[at_i] = 0.5 * (Y2[at_i] + YP[at_i].astype(F32)) + F2[at_i] - G2[at_i]
        y_out(i).start()
        return carry

    lax.fori_loop(0, NCHUNK, track, 0)

    def swaps_end(i, carry):
        p_copy(i).wait_send()
        y_copy(i).wait_send()
        y_out(i).wait()
        return carry

    lax.fori_loop(0, NCHUNK, swaps_end, 0)

    def slots_end(s, carry):
        norm_core(s).wait_send()
        norm_side(s).wait_send()
        norm_far(s).wait_send()
        near_copy(s, 0).wait_send()
        near_copy(s, 1).wait_send()
        far_copy(s).wait_send()
        return carry

    lax.fori_loop(0, SLOTS, slots_end, 0)
    for wait in ends:
        wait()
    q_out.wait()
    if first:
        f_out.wait()


def iteration(t, hop, state, images, cot, ids, counts):
    first = t == 0
    pm, pc, pb, ym, yc, yb, gm, gc, gb = state
    hbm = pl.BlockSpec(memory_space=pl.ANY)
    vmem = pl.BlockSpec(memory_space=pltpu.VMEM)
    smem = pl.BlockSpec(memory_space=pltpu.SMEM)
    ins = [("images", images, hbm), ("ids", ids, smem)] if first else [("picked", images, vmem)]
    ins += [("counts", counts, smem), ("cot", cot, hbm)]
    ins += [("pm", pm, hbm), ("pc", pc, vmem), ("pb", pb, vmem)]
    ins += [("ym", ym, hbm), ("yc", yc, vmem), ("yb", yb, vmem)]
    ins += [("gm", gm, hbm), ("gc", gc, vmem), ("gb", gb, vmem)]
    outs = [("qm", pm, hbm), ("qc", pc, vmem), ("qb", pb, vmem)]
    outs += [("new_ym", ym, hbm), ("new_yc", yc, vmem), ("new_yb", yb, vmem)]
    if first:
        outs += [("fm", gm, hbm), ("fc", gc, vmem), ("fb", gb, vmem)]
        outs += [("picked_next", jax.ShapeDtypeStruct((SLOTS, SIDE, SIDE, CW), BF16), vmem)]
    V = pltpu.VMEM
    mats = (2, C, HID)
    maps = (SIDE, SIDE, CW)
    scratch = {n: V(mats, F32) for n in ("P2", "Y2", "G2", "F2")}
    scratch |= {n: V(mats, BF16) for n in ("PB", "PP", "YB", "YP", "W")}
    scratch |= {n: V((ROWS, C), BF16) for n in ("NF", "CF", "DB", "ACT", "DH")}
    scratch |= {n: V((ROWS, CW), F32) for n in ("X", "INV", "DN")}
    scratch |= {n: V((ROWS, CW), BF16) for n in ("S2", "R2")}
    scratch |= {n: V((SLOTS, SIDE, PADW, CW), F32) for n in ("CP", "DC")}
    scratch |= {n: V((NCHAN, 8, STATW), F32) for n in ("STR", "BS", "BR")}
    scratch |= {n: V((TAPS + 5, CW), F32) for n in ("RPC", "RYC")}
    scratch |= {n: V((1, HID), F32) for n in ("RPB", "RYB", "GB")}
    scratch |= {
        "DP": V((ROWS, C), F32),
        "R1": V((2, ROWS, CW), F32),
        "GS": V((NCHAN, 8, CW), F32),
        "FC": V((TAPS + 7, CW), F32),
        "XP": V((SLOTS, SIDE + 6, 24, CW), F32),
        "SH": V((KS, SLOTS, SIDE + 6, PADW, CW), F32),
        "COTL": V((SLOTS,) + maps, BF16),
        "send": pltpu.SemaphoreType.DMA((96,)),
        "recv": pltpu.SemaphoreType.DMA((96,)),
        "local": pltpu.SemaphoreType.DMA((32,)),
    }
    if first:
        scratch |= {
            "G0": V((16,) + maps, BF16),
            "G1": V((16,) + maps, BF16),
            "XS": V((2, 3, SLOTS) + maps, BF16),
            "XR0": V((4, SLOTS) + maps, BF16),
            "XR1": V((4, SLOTS) + maps, BF16),
            "IDV": V((4, 8, 128), jnp.int32),
            "IDS": pltpu.SMEM((4, 8, 128), jnp.int32),
        }
    names = [n for n, _, _ in ins] + [n for n, _, _ in outs] + list(scratch)
    return pl.pallas_call(
        functools.partial(kernel, t, hop, names),
        out_shape=[jax.ShapeDtypeStruct(a.shape, a.dtype) for _, a, _ in outs],
        in_specs=[s for _, _, s in ins],
        out_specs=[s for _, _, s in outs],
        scratch_shapes=list(scratch.values()),
        compiler_params=pltpu.CompilerParams(
            collective_id=t * 3 + hop,
            has_side_effects=True,
            vmem_limit_bytes=58 * 1024 * 1024,
        ),
    )(*[a for _, a, _ in ins])


def on_device(images, cotangent, image_ids, counts, hop_exponents, *state):
    def branch(t, hop):
        def run(operands):
            source, state = operands
            return iteration(t, hop, state, source, cotangent, image_ids, counts)

        return run

    def step(t, source, state):
        return lax.switch(
            jnp.clip(hop_exponents[t], 0, 2), [branch(t, hop) for hop in range(3)], (source, state)
        )

    out = step(0, images, state)
    return tuple(step(1, out[9], tuple(out[:9])))


def solution(mesh):
    mats, chans, bias = P("peer", None, None, "chan"), P("peer", None, "chan"), P("peer", "chan")
    in_specs = (
        P(None, "peer", None, None, "chan"),
        P(None, "peer", None, None, None, "chan"),
        P(None, "peer", None),
        P(None, "peer"),
        P(),
    ) + (mats, chans, bias) * 3
    return jax.shard_map(
        on_device, mesh=mesh, in_specs=in_specs, out_specs=(mats, chans, bias) * 2, check_vma=False
    )
```

time: 662 us -> 195 us (0.29)
  waiting for transfers between devices: 292 us -> 0 us
  Pallas kernels: 0 us -> 164 us
  local copies, waits for them, and re-layouts: 156 us -> 19.1 us
  other arithmetic: 82.2 us -> 0 us
  blocking collectives: 73.1 us -> 0 us
  matrix products: 30.5 us -> 0 us
  between operations: 18.2 us -> 1.99 us
  loops' own time: 0.42 us -> 8.55 us
    ppermute x2 -> x0, waiting for transfers between devices: 194 us -> none  [partner(): lax.ppermute(value, axis, [(i, i ^ 1 << stride) for i in range(lax.axis_s...]
    pallas_call x0 -> x2, Pallas kernels: none -> 164 us  [iteration(): pl.pallas_call(functools.partial(kernel, t, hop, names), out_shape=[jax.S...]
    slice x21 -> x1, local copies, waits for them, and re-layouts: 64.3 us -> 1.31 us  [step(): hop_exponents[t]]
    reduce_scatter x4 -> x0, waiting for transfers between devices: 54.5 us -> none  [the longest x2 39.2 us: local_grad(): lax.psum_scatter(partial_out, 'chan', scatter_dimension=1, tiled=True)]
    all_gather x2 -> x0, waiting for transfers between devices: 43 us -> none  [fetch_images(): piece = lax.all_gather(flat_images, 'peer', axis=0, tiled=True)]
    all_gather x4 -> x0, blocking collectives: 37.3 us -> none  [the longest x2 19 us: local_grad(): normed_full = lax.all_gather(normalized_rows, 'chan', axis=1, tiled=True)]
    unnamed x123 -> x10, local copies, waits for them, and re-layouts: 40.8 us -> 4.25 us
    psum x6 -> x0, blocking collectives: 35.9 us -> none  [the longest x2 13.1 us: local_grad(): average = lax.psum(jnp.sum(conv_out, 1), 'chan') / full_width]
  transfers between devices with their start and end apart: 8 -> 0, of which waited for: 7 -> 0; matrix products, arithmetic and copies ran while one was open for 20% -> 0% of each run, Pallas kernels for 0% -> 0%
where the time goes in v1:
time: 195 us; the launch traced here: 194 us
  Pallas kernels  164 us (84%)
  local copies, waits for them, and re-layouts  19.1 us (10%)
  loops' own time  8.55 us (4%)
  between operations  1.99 us (1%)
    pallas_call x2, Pallas kernels, iteration(): pl.pallas_call(functools.partial(kernel, t, hop, names), out_shape=[jax.S...  164 us
    another operation x8, local copies, waits for them, and re-layouts  12 us
    another operation x2, loops' own time, step(): lax.switch(jnp.clip(hop_exponents[t], 0, 2), [branch(t, hop) for hop in r...  8.55 us
    unnamed x10, local copies, waits for them, and re-layouts  4.25 us

profile of v1, /device:TPU:1, one launch (start us, length us, event | category | flops | bytes accessed | tf_op | source)
XLA Modules:
  0.0 193.8 jit_solution(18032335966213383456)
XLA Ops:
  0.6 1.3 fusion
  3.3 125.5 %conditional.2 = ((f32[1,2,512,512]{3,2,1,0:T(8,128)S(1)}, f32[1,54,128]{2,1,0:T(8,128)S(1)}, f32[1,512]{1,0:T(1,128)S(1)}, f32[1,2,512,512]{3,2,1,0:T(8,128)}, ...) conditional(s32[]{:T(128)} %bitcast.1, ...), branch_computations={%region_0.1_spmd, %region_1.2_spmd, %region_2.3_spmd} | conditional | bytes 1370136 | solution.py:620
  3.3 1.3 copy.39.refs_2_
  4.6 1.3 copy.43.refs_11_
  5.9 1.3 copy.42.refs_8_
  7.3 1.3 copy.41.refs_5_
  8.6 1.6 copy.38.refs_0_
  10.3 1.8 copy.40.refs_3_
  12.1 108.5 %branch_0_fun.2 = (f32[1,2,512,512]{3,2,1,0:T(8,128)S(1)}, f32[1,54,128]{2,1,0:T(8,128)S(1)}, f32[1,512]{1,0:T(1,128)S(1)}, f32[1,2,512,512]{3,2,1,0:T(8,128)}, ...) custom-call(bf16[2,2,14,14,128]{4,3,2,1,0:T(8,128)(2,1)} %copy.38.re, ...), custom_call_target="tpu_custom_call" | custom-call | tf_op jit(solution)/shard_map/cond/branch_0_fun/pallas_call | solution.py:597
  128.8 60.7 %conditional.3 = (f32[1,2,512,512]{3,2,1,0:T(8,128)S(1)}, f32[1,512]{1,0:T(1,128)S(1)}, f32[1,2,512,512]{3,2,1,0:T(8,128)}, f32[1,512]{1,0:T(1,128)S(1)}, f32[1,...) conditional(s32[]{:T(128)} %bitcast, (bf16[4,14,14,128]{3,2,1,0:T(8,128)(2,1)S(1)}, ...), branch_computations={%region_3.4_spmd, %region_4.5_spmd, %region_5.6_spmd} | conditional | bytes 913472 | solution.py:620
  128.8 1.3 copy.58.refs_1_
  130.1 1.8 copy.59.refs_2_
  132.0 55.6 %branch_1_fun.3 = (f32[1,2,512,512]{3,2,1,0:T(8,128)S(1)}, f32[1,54,128]{2,1,0:T(8,128)}, f32[1,512]{1,0:T(1,128)S(1)}, f32[1,2,512,512]{3,2,1,0:T(8,128)}, f32[1,54,128]{2,1,0:T(8,128)}, /*index=5*/f32[1,512]{1,0:T(1,128)S(1)}) custom-call(bf16[4,14,14,128]{3,2,1,0:T(8,128)(2,1)S(1)} %get-tuple-element.201.refs_0_, s32[2,1]{1,0:T(2,128)} %copy.58.refs_1_, ...), custom_call_target="tpu_custom_call" | custom-call | tf_op jit(solution)/shard_map/cond/branch_1_fun/pallas_call | solution.py:597
  187.6 0.8 copy.65
  188.4 0.8 copy.68
  189.5 0.0 copy-start.1
  189.5 0.0 copy-start.2
  189.5 0.0 copy-start
  189.6 1.3 copy.122
  190.9 0.0 copy-done.1
  190.9 0.0 copy-done.2
  190.9 0.6 copy.123
  191.5 0.4 copy-done
  191.9 1.3 copy.124
  193.2 0.6 copy.125
Async XLA Ops:
  189.5 1.4 copy-start.1
  189.5 1.3 copy-start.2
  189.5 2.4 %copy-start = (f32[1,2,512,512]{3,2,1,0:T(8,128)S(1)}, f32[1,2,512,512]{3,2,1,0:T(8,128)}, u32[]{:S(2)}) copy-start(f32[1,2,512,512]{3,2,1,0:T(8,128)} %get-tuple-element.435) | copy-start | bytes 6291460
